TPU v7x, 32 devices: a whole 2x2x4 slice. The times are simulated.
32 devices in a mesh: groups: 2 (over x), seq: 16 (over z, y, core).
Axes of the slice: x: 2, y: 2, z: 4, core: 2. Of those that a mesh axis runs over, the one named last changes fastest.
Arguments:
- q_tokens: bfloat16 [4096, 2048], P(('groups', 'seq')), parts along dimension 0, may hold values from -44 to 44
- k_tokens: bfloat16 [4096, 2048], P(('groups', 'seq')), parts along dimension 0, may hold values from -4 to 4
- v_tokens: bfloat16 [4096, 2048], P(('groups', 'seq')), parts along dimension 0, may hold values from -6 to 6
- dout_tokens: bfloat16 [4096, 2048], P(('groups', 'seq')), parts along dimension 0, may hold values from -6 to 6
- q_beacons: bfloat16 [128, 2048], P(('groups', 'seq')), parts along dimension 0, may hold values from -44 to 44
- k_beacons: bfloat16 [128, 2048], P(('groups', 'seq')), parts along dimension 0, may hold values from -4 to 4
- v_beacons: bfloat16 [128, 2048], P(('groups', 'seq')), parts along dimension 0, may hold values from -6 to 6
- dout_beacons: bfloat16 [128, 2048], P(('groups', 'seq')), parts along dimension 0, may hold values from -6 to 6
- block_mask: int32 [32, 16], P(('groups', 'seq')), parts along dimension 0, may hold values 0 or 1
- beacon_offsets: int32 [128], P(('groups', 'seq')), parts along dimension 0, may hold values from 0 to 31
Outputs:
- out_tokens: bfloat16 [4096, 2048], P(('groups', 'seq')), parts along dimension 0
- out_beacons: bfloat16 [128, 2048], P(('groups', 'seq')), parts along dimension 0
- grad_q_tokens: bfloat16 [4096, 2048], P(('groups', 'seq')), parts along dimension 0
- grad_k_tokens: bfloat16 [4096, 2048], P(('groups', 'seq')), parts along dimension 0
- grad_v_tokens: bfloat16 [4096, 2048], P(('groups', 'seq')), parts along dimension 0
- grad_q_beacons: bfloat16 [128, 2048], P(('groups', 'seq')), parts along dimension 0
- grad_k_beacons: bfloat16 [128, 2048], P(('groups', 'seq')), parts along dimension 0
- grad_v_beacons: bfloat16 [128, 2048], P(('groups', 'seq')), parts along dimension 0
There are 2 independent parts, one for each index of `groups`. A program takes and returns all parts, laid end to end along the dimension named above; each array names one. Nothing has to cross between parts.
All inputs are finite; a program needn't handle non-finite values. No bound on the sum of `block_mask` on one device may be relied on, other than what follows from the above.
Results may differ from a plain program's by a relative error of at most 0.015.
The roundings to bfloat16 on the way count: a program that leaves them out, or rounds other values in their place, can miss the bound.
Values may be sent and summed in bfloat16 or wider, within the bound.
A program may use at most 128 MiB of HBM per device.

v0:
```python
import jax
import jax.numpy as jnp
from jax import lax
from jax.sharding import PartitionSpec as P

HEAD_DIM = 128


def passed_along(value, axis, steps):
    count = lax.axis_size(axis)
    first, last = (max(0, -steps), min(count, count - steps))
    return lax.ppermute(value, axis, [(source, source + steps) for source in range(first, last)])


def visible(seg_index, mask_row, offsets, seg_len, beacon_count, window, segments):
    ratio = seg_len // beacon_count
    rows_total = seg_len + beacon_count
    query_ids = jnp.arange(rows_total, dtype=jnp.int32)[:, None]
    is_raw = query_ids < seg_len
    beacon_id = query_ids - seg_len
    limit = jnp.concatenate(
        [
            jnp.zeros((seg_len,), jnp.int32),
            jnp.arange(beacon_count, dtype=jnp.int32) * ratio + offsets,
        ]
    )[:, None]
    key_ids = jnp.arange(window + seg_len + segments * beacon_count, dtype=jnp.int32)[None, :]
    in_window = key_ids < window
    in_own = (key_ids >= window) & (key_ids < window + seg_len)
    lag_own = query_ids - (key_ids - window)
    flat_id = key_ids - window - seg_len
    owner = flat_id // beacon_count
    slot_id = flat_id % beacon_count
    opened = (
        jnp.concatenate(
            [jnp.zeros((window + seg_len,), jnp.int32), jnp.repeat(mask_row, beacon_count)]
        )[None, :]
        == 1
    )
    earlier = (flat_id >= 0) & (owner < seg_index) & opened
    raw_ok = (
        in_window & (key_ids > query_ids) & (seg_index >= 1)
        | in_own & (lag_own >= 0) & (lag_own < window)
        | earlier
    )
    beacon_ok = (
        in_own & (key_ids - window <= limit)
        | earlier
        | (flat_id >= 0) & (owner == seg_index) & (slot_id <= beacon_id)
    )
    return jnp.where(is_raw, raw_ok, beacon_ok)


def attend(queries, key_rows, values, grads_out, allowed, score_scale):
    scores = (
        jnp.einsum("qhd,khd->hqk", queries, key_rows, preferred_element_type=jnp.float32)
        * score_scale
    )
    scores = jnp.where(allowed[None], scores, -jnp.inf)
    row_max = jnp.max(scores, axis=2, keepdims=True)
    exp_scores = jnp.exp(scores - row_max)
    prob_rows = exp_scores / jnp.sum(exp_scores, axis=2, keepdims=True)
    weights = prob_rows.astype(jnp.bfloat16)
    output = jnp.einsum("hqk,khd->qhd", weights, values, preferred_element_type=jnp.float32).astype(
        jnp.bfloat16
    )
    out_kept = lax.optimization_barrier(output)
    row_delta = jnp.sum(grads_out.astype(jnp.float32) * out_kept.astype(jnp.float32), axis=2)
    grad_prob = jnp.einsum("qhd,khd->hqk", grads_out, values, preferred_element_type=jnp.float32)
    dscores = (prob_rows * (grad_prob - row_delta.T[:, :, None])).astype(jnp.bfloat16)
    grad_q = (
        jnp.einsum("hqk,khd->qhd", dscores, key_rows, preferred_element_type=jnp.float32)
        * score_scale
    ).astype(jnp.bfloat16)
    grad_k = (
        jnp.einsum("hqk,qhd->khd", dscores, queries, preferred_element_type=jnp.float32)
        * score_scale
    )
    grad_v = jnp.einsum("hqk,qhd->khd", weights, grads_out, preferred_element_type=jnp.float32)
    return (output, grad_q, grad_k, grad_v)


def heads_view(matrix, col_lo, block_heads):
    return matrix[:, col_lo : col_lo + block_heads * HEAD_DIM].reshape(
        matrix.shape[0], block_heads, HEAD_DIM
    )


def per_device(
    q_tokens,
    k_tokens,
    v_tokens,
    dout_tokens,
    q_beacons,
    k_beacons,
    v_beacons,
    dout_beacons,
    block_mask,
    beacon_offsets,
):
    seg_len = q_tokens.shape[0]
    feat_width = q_tokens.shape[1]
    beacon_count = q_beacons.shape[0]
    window = seg_len // 2
    segments = lax.axis_size("seq")
    seg_index = lax.axis_index("seq")
    score_scale = 1.0 / HEAD_DIM**0.5
    tail_k, tail_v = passed_along(
        (k_tokens[seg_len - window :], v_tokens[seg_len - window :]), "seq", 1
    )
    every_bk, every_bv = (
        lax.all_gather(k_beacons, "seq", axis=0, tiled=True),
        lax.all_gather(v_beacons, "seq", axis=0, tiled=True),
    )
    queries = jnp.concatenate([q_tokens, q_beacons], axis=0)
    key_rows = jnp.concatenate([tail_k, k_tokens, every_bk], axis=0)
    values = jnp.concatenate([tail_v, v_tokens, every_bv], axis=0)
    grads_out = jnp.concatenate([dout_tokens, dout_beacons], axis=0)
    allowed = visible(
        seg_index, block_mask[0], beacon_offsets, seg_len, beacon_count, window, segments
    )
    heads_total = feat_width // HEAD_DIM
    block_heads = 4
    out_parts, gq_parts, gk_parts, gv_parts = ([], [], [], [])
    for group in range(heads_total // block_heads):
        col_lo = group * block_heads * HEAD_DIM
        output, grad_q, grad_k, grad_v = attend(
            heads_view(queries, col_lo, block_heads),
            heads_view(key_rows, col_lo, block_heads),
            heads_view(values, col_lo, block_heads),
            heads_view(grads_out, col_lo, block_heads),
            allowed,
            score_scale,
        )
        out_parts.append(output.reshape(output.shape[0], -1))
        gq_parts.append(grad_q.reshape(grad_q.shape[0], -1))
        gk_parts.append(grad_k.reshape(grad_k.shape[0], -1))
        gv_parts.append(grad_v.reshape(grad_v.shape[0], -1))
    out_all = jnp.concatenate(out_parts, axis=1)
    gq_all = jnp.concatenate(gq_parts, axis=1)
    gk_all = jnp.concatenate(gk_parts, axis=1)
    gv_all = jnp.concatenate(gv_parts, axis=1)
    back_k, back_v = (
        passed_along(gk_all[:window].astype(jnp.bfloat16), "seq", -1).astype(jnp.float32),
        passed_along(gv_all[:window].astype(jnp.bfloat16), "seq", -1).astype(jnp.float32),
    )
    own_k = gk_all[window : window + seg_len]
    own_v = gv_all[window : window + seg_len]
    grad_k_tokens = jnp.concatenate(
        [own_k[: seg_len - window], own_k[seg_len - window :] + back_k], axis=0
    ).astype(jnp.bfloat16)
    grad_v_tokens = jnp.concatenate(
        [own_v[: seg_len - window], own_v[seg_len - window :] + back_v], axis=0
    ).astype(jnp.bfloat16)
    beacon_k_terms = gk_all[window + seg_len :]
    beacon_v_terms = gv_all[window + seg_len :]
    total_k, total_v = (
        lax.psum_scatter(beacon_k_terms, "seq", scatter_dimension=0, tiled=True),
        lax.psum_scatter(beacon_v_terms, "seq", scatter_dimension=0, tiled=True),
    )
    return (
        out_all[:seg_len],
        out_all[seg_len:],
        gq_all[:seg_len],
        grad_k_tokens,
        grad_v_tokens,
        gq_all[seg_len:],
        total_k.astype(jnp.bfloat16),
        total_v.astype(jnp.bfloat16),
    )


def solution(mesh):
    placed = (
        P(("groups", "seq"), None),
        P(("groups", "seq"), None),
        P(("groups", "seq"), None),
        P(("groups", "seq"), None),
        P(("groups", "seq"), None),
        P(("groups", "seq"), None),
        P(("groups", "seq"), None),
        P(("groups", "seq"), None),
        P(("groups", "seq"), None),
        P(("groups", "seq")),
    )
    return jax.shard_map(
        per_device,
        mesh=mesh,
        in_specs=placed,
        out_specs=(
            P(("groups", "seq"), None),
            P(("groups", "seq"), None),
            P(("groups", "seq"), None),
            P(("groups", "seq"), None),
            P(("groups", "seq"), None),
            P(("groups", "seq"), None),
            P(("groups", "seq"), None),
            P(("groups", "seq"), None),
        ),
        check_vma=False,
    )
```

profile of v0, /device:TPU:0, one launch (start us, length us, event | category | flops | bytes accessed | tf_op | source)
XLA Modules:
  0.0 191.9 jit_solution(11802820695143670854)
XLA Ops:
  0.7 1.4 copy.145
  3.1 3.3 %collective-permute-start.1 = (bf16[64,2048]{0,1:T(8,128)(2,1)}, bf16[64,2048]{0,1:T(8,128)(2,1)}, u32[]{:S(2)}, u32[]{:S(2)}) collective-permute-start(bf16[64,2048]{0,1:T(8,128)(2,1)} %slice.133), channel_id=1, source_target_pairs={{0,1},{1,2},{2,3},{3,4},{4,5},{5,6},{6,7},{7,8},{8,9},{9,10},{10,1... | collective-permute-start | bytes 786440 | tf_op jit(solution)/shard_map/ppermute | solution.py:12
  7.7 4.7 %collective-permute-start = (bf16[64,2048]{0,1:T(8,128)(2,1)}, bf16[64,2048]{0,1:T(8,128)(2,1)}, u32[]{:S(2)}, u32[]{:S(2)}) collective-permute-start(bf16[64,2048]{0,1:T(8,128)(2,1)} %slice.130), channel_id=1, source_target_pairs={{0,1},{1,2},{2,3},{3,4},{4,5},{5,6},{6,7},{7,8},{8,9},{9,10},{10,1... | collective-permute-start | bytes 786440 | tf_op jit(solution)/shard_map/ppermute | solution.py:12
  12.5 22.0 %all-gather.1 = bf16[16,4,2048]{2,1,0:T(4,128)(2,1)S(1)} all-gather(bf16[1,4,2048]{2,1,0:T(4,128)(2,1)S(1)} %bitcast.160), channel_id=1, replica_groups=mesh['groups'=2,'seq'=16] {'seq'}, dimensions={0}, use_global_device_ids=true | all-gather | bytes 278528 | tf_op jit(solution)/shard_map/all_gather | solution.py:112
  34.6 20.0 %all-gather = bf16[16,4,2048]{2,1,0:T(4,128)(2,1)S(1)} all-gather(bf16[1,4,2048]{2,1,0:T(4,128)(2,1)S(1)} %bitcast.161), channel_id=1, replica_groups=mesh['groups'=2,'seq'=16] {'seq'}, dimensions={0}, use_global_device_ids=true | all-gather | bytes 278528 | tf_op jit(solution)/shard_map/all_gather | solution.py:113
  61.6 1.6 pad_maximum_fusion.3
  63.3 1.6 pad_maximum_fusion.2
  67.9 2.0 %fusion.68 = f32[4,128,256]{2,1,0:T(8,128)} fusion(bf16[132,4,128]{2,1,0:T(4,128)(2,1)S(1)} %reshape.434, f32[4,132]{1,0:T(4,128)S(1)} %get-tuple-element.34, bf16[256,4,128]{0,2,1:T(8,128)(2,1)S(1)} %bitcast.130, pred[132,256]{1,0:T(8,128)(4,1)S(1)} %fusion.48, bf16[132,4,128]{2,1,0:T(4,128)(2,1)S(1)} %reshape.419), kind=kOutput, calls=%fused_computation.106 | convolution fusion | flops 69882640 | bytes 1092672 | tf_op jit(solution)/shard_map/hqk,qhd->khd/dot_general | solution.py:79
  70.2 1.3 fusion.20
  74.2 2.0 %fusion.65 = f32[4,128,256]{2,1,0:T(8,128)} fusion(bf16[132,4,128]{2,1,0:T(4,128)(2,1)S(1)} %reshape.436, f32[4,132]{1,0:T(4,128)S(1)} %get-tuple-element.36, bf16[256,4,128]{0,2,1:T(8,128)(2,1)S(1)} %bitcast.126, pred[132,256]{1,0:T(8,128)(4,1)S(1)} %fusion.48, bf16[132,4,128]{2,1,0:T(4,128)(2,1)S(1)} %reshape.423), kind=kOutput, calls=%fused_computation.103 | convolution fusion | flops 69882640 | bytes 1092672 | tf_op jit(solution)/shard_map/hqk,qhd->khd/dot_general | solution.py:79
  76.5 1.3 fusion.21
  80.5 2.0 %fusion.62 = f32[4,128,256]{2,1,0:T(8,128)} fusion(bf16[132,4,128]{2,1,0:T(4,128)(2,1)S(1)} %reshape.438, f32[4,132]{1,0:T(4,128)S(1)} %get-tuple-element.38, bf16[256,4,128]{0,2,1:T(8,128)(2,1)S(1)} %bitcast.122, pred[132,256]{1,0:T(8,128)(4,1)S(1)} %fusion.48, bf16[132,4,128]{2,1,0:T(4,128)(2,1)S(1)} %reshape.427), kind=kOutput, calls=%fused_computation.100 | convolution fusion | flops 69882640 | bytes 1092672 | tf_op jit(solution)/shard_map/hqk,qhd->khd/dot_general | solution.py:79
  82.7 1.3 fusion.22
  85.7 2.0 %fusion.31 = bf16[132,4,128]{2,0,1:T(8,128)(2,1)S(1)} fusion(bf16[256,4,128]{0,2,1:T(8,128)(2,1)} %bitcast.152, f32[4,132]{1,0:T(4,128)S(1)} %get-tuple-element.40, bf16[256,4,128]{0,2,1:T(8,128)(2,1)S(1)} %bitcast.117, pred[132,256]{1,0:T(8,128)(4,1)S(1)} %fusion.48, bf16[132,4,128]{2,1,0:T(4,128)(2,1)S(1)} %reshape.431), kind=kOutput, calls=%fused_computation.53 | convolution fusion | flops 69950224 | bytes 830528 | tf_op jit(solution)/shard_map/hqk,khd->qhd/dot_general | solution.py:64
  92.8 2.0 %fusion.59 = f32[4,128,256]{2,1,0:T(8,128)} fusion(bf16[132,4,128]{2,1,0:T(4,128)(2,1)S(1)} %reshape.440, f32[4,132]{1,0:T(4,128)S(1)} %get-tuple-element.40, bf16[256,4,128]{0,2,1:T(8,128)(2,1)S(1)} %bitcast.119, pred[132,256]{1,0:T(8,128)(4,1)S(1)} %fusion.48, bf16[132,4,128]{2,1,0:T(4,128)(2,1)S(1)} %reshape.431), kind=kOutput, calls=%fused_computation.97 | convolution fusion | flops 69882640 | bytes 1092672 | tf_op jit(solution)/shard_map/hqk,qhd->khd/dot_general | solution.py:79
  98.4 1.4 pad_maximum_fusion
  99.8 1.2 copy.196
  102.2 2.0 %copy.198 = f32[256,512]{1,0:T(8,128)} copy(f32[256,512]{0,1:T(8,128)} %bitcast.150) | data formatting | bytes 1048576 | tf_op jit(solution)/shard_map/reshape | solution.py:138
  104.3 2.0 %copy.199 = f32[256,512]{1,0:T(8,128)} copy(f32[256,512]{0,1:T(8,128)} %bitcast.151) | data formatting | bytes 1048576 | tf_op jit(solution)/shard_map/reshape | solution.py:138
  107.4 1.4 collective-permute-start.2
  108.8 1.3 fusion.141
  110.9 1.3 collective-permute-start.3
  112.5 2.4 %collective-permute-done.3 = bf16[64,2048]{1,0:T(8,128)(2,1)S(1)} collective-permute-done((bf16[64,2048]{1,0:T(8,128)(2,1)S(1)}, bf16[64,2048]{1,0:T(8,128)(2,1)S(1)}, u32[]{:S(2)}, u32[]{:S(2)}) %collective-permute-start.3) | collective-permute-done | bytes 262176 | tf_op jit(solution)/shard_map/ppermute | solution.py:12
  115.1 73.9 %all-reduce.6 = (bf16[64,2048]{1,0:T(8,128)(2,1)S(1)}, bf16[64,2048]{1,0:T(8,128)(2,1)S(1)}) all-reduce(f32[64,2048]{1,0:T(8,128)S(1)} %get-tuple-element.12, f32[64,2048]{1,0:T(8,128)S(1)} %get-tuple-element.10), channel_id=2, replica_groups=mesh['groups'=2,'seq'=16] {'seq'}, use_global_device_ids=true, to_apply=%region_12.13.clone | all-reduce | flops 262144 | bytes 1572864
  (140 shorter events, 34.2 us)
Async XLA Ops:
  0.6 5.7 %copy-start.5 = (bf16[128,2048]{1,0:T(8,128)(2,1)S(1)}, bf16[128,2048]{1,0:T(8,128)(2,1)}, u32[]{:S(2)}) copy-start(bf16[128,2048]{1,0:T(8,128)(2,1)} %param.12) | copy-start | bytes 1572868
  0.6 11.7 %copy-start.13 = (s32[4]{0:T(128)S(1)}, s32[4]{0:T(128)}, u32[]{:S(2)}) copy-start(s32[4]{0:T(128)} %param.19) | copy-start | bytes 52
  0.7 11.7 %copy-start.12 = (s32[1,16]{1,0:T(1,128)S(1)}, s32[1,16]{1,0:T(1,128)}, u32[]{:S(2)}) copy-start(s32[1,16]{1,0:T(1,128)} %param.18) | copy-start | bytes 196
  0.7 11.9 %copy-start.8 = (bf16[4,2048]{1,0:T(4,128)(2,1)S(1)}, bf16[4,2048]{1,0:T(4,128)(2,1)}, u32[]{:S(2)}) copy-start(bf16[4,2048]{1,0:T(4,128)(2,1)} %param.15) | copy-start | bytes 49156
  0.7 33.9 %copy-start.9 = (bf16[4,2048]{1,0:T(4,128)(2,1)S(1)}, bf16[4,2048]{1,0:T(4,128)(2,1)}, u32[]{:S(2)}) copy-start(bf16[4,2048]{1,0:T(4,128)(2,1)} %param.16) | copy-start | bytes 49156
  2.1 52.5 %copy-start.6 = (bf16[128,2048]{1,0:T(8,128)(2,1)S(1)}, bf16[128,2048]{1,0:T(8,128)(2,1)}, u32[]{:S(2)}) copy-start(bf16[128,2048]{1,0:T(8,128)(2,1)} %param.10) | copy-start | bytes 1572868
  3.1 51.6 %copy-start.10 = (bf16[4,2048]{1,0:T(4,128)(2,1)S(1)}, bf16[4,2048]{1,0:T(4,128)(2,1)}, u32[]{:S(2)}) copy-start(bf16[4,2048]{1,0:T(4,128)(2,1)} %param.14) | copy-start | bytes 49156
  3.1 58.5 %collective-permute-start.1 = (bf16[64,2048]{0,1:T(8,128)(2,1)}, bf16[64,2048]{0,1:T(8,128)(2,1)}, u32[]{:S(2)}, u32[]{:S(2)}) collective-permute-start(bf16[64,2048]{0,1:T(8,128)(2,1)} %slice.133), channel_id=1, source_target_pairs={{0,1},{1,2},{2,3},{3,4},{4,5},{5,6},{6,7},{7,8},{8,9},{9,10},{10,1... | collective-permute-start | bytes 786440 | tf_op jit(solution)/shard_map/ppermute | solution.py:12
  7.6 48.8 %copy-start.11 = (bf16[4,2048]{1,0:T(4,128)(2,1)S(1)}, bf16[4,2048]{1,0:T(4,128)(2,1)}, u32[]{:S(2)}) copy-start(bf16[4,2048]{1,0:T(4,128)(2,1)} %param.17) | copy-start | bytes 49156
  7.7 55.7 %collective-permute-start = (bf16[64,2048]{0,1:T(8,128)(2,1)}, bf16[64,2048]{0,1:T(8,128)(2,1)}, u32[]{:S(2)}, u32[]{:S(2)}) collective-permute-start(bf16[64,2048]{0,1:T(8,128)(2,1)} %slice.130), channel_id=1, source_target_pairs={{0,1},{1,2},{2,3},{3,4},{4,5},{5,6},{6,7},{7,8},{8,9},{9,10},{10,1... | collective-permute-start | bytes 786440 | tf_op jit(solution)/shard_map/ppermute | solution.py:12
  57.4 2.8 %copy-start.14 = (u32[32]{0:T(128)S(1)}, u32[32]{0:T(128)}, u32[]{:S(2)}) copy-start(u32[32]{0:T(128)} %constant.76) | copy-start | bytes 388
  88.2 2.4 %copy-start.7 = (bf16[256,512]{0,1:T(8,128)(2,1)S(1)}, bf16[256,512]{0,1:T(8,128)(2,1)}, u32[]{:S(2)}) copy-start(bf16[256,512]{0,1:T(8,128)(2,1)} %get-tuple-element.22) | copy-start | bytes 786436
  88.2 2.4 %copy-start.15 = (f32[4,132,256]{2,1,0:T(8,128)S(1)}, f32[4,132,256]{2,1,0:T(8,128)}, u32[]{:S(2)}) copy-start(f32[4,132,256]{2,1,0:T(8,128)} %get-tuple-element.41) | copy-start | bytes 1622020
  95.7 0.8 copy-start.2
  96.5 0.8 copy-start.3
  107.4 4.8 %copy-start = (f32[256,512]{1,0:T(8,128)S(1)}, f32[256,512]{1,0:T(8,128)}, u32[]{:S(2)}) copy-start(f32[256,512]{1,0:T(8,128)} %copy.198) | copy-start | bytes 1572868
  107.4 4.8 %copy-start.1 = (f32[256,512]{1,0:T(8,128)S(1)}, f32[256,512]{1,0:T(8,128)}, u32[]{:S(2)}) copy-start(f32[256,512]{1,0:T(8,128)} %copy.199) | copy-start | bytes 1572868
  107.4 5.0 %collective-permute-start.2 = (bf16[64,2048]{1,0:T(8,128)(2,1)S(1)}, bf16[64,2048]{1,0:T(8,128)(2,1)S(1)}, u32[]{:S(2)}, u32[]{:S(2)}) collective-permute-start(bf16[64,2048]{1,0:T(8,128)(2,1)S(1)} %get-tuple-element.17), channel_id=1, source_target_pairs={{1,0},{2,1},{3,2},{4,3},{5,4},{6,5},{7,6},{8,7},{9,8},{10,9},{11,1... | collective-permute-start | bytes 786440 | tf_op jit(solution)/shard_map/ppermute | solution.py:12
  110.9 4.0 %collective-permute-start.3 = (bf16[64,2048]{1,0:T(8,128)(2,1)S(1)}, bf16[64,2048]{1,0:T(8,128)(2,1)S(1)}, u32[]{:S(2)}, u32[]{:S(2)}) collective-permute-start(bf16[64,2048]{1,0:T(8,128)(2,1)S(1)} %get-tuple-element.15), channel_id=1, source_target_pairs={{1,0},{2,1},{3,2},{4,3},{5,4},{6,5},{7,6},{8,7},{9,8},{10,9},{11,1... | collective-permute-start | bytes 786440 | tf_op jit(solution)/shard_map/ppermute | solution.py:12
  112.5 78.5 %copy-start.4 = (bf16[64,2048]{1,0:T(8,128)(2,1)S(1)}, bf16[64,2048]{1,0:T(8,128)(2,1)}, u32[]{:S(2)}) copy-start(bf16[64,2048]{1,0:T(8,128)(2,1)} %get-tuple-element.14) | copy-start | bytes 786436
where the time goes:
time: 193 us; the launch traced here: 192 us
  blocking collectives  116 us (60%)
  local copies, waits for them, and re-layouts  26.5 us (14%)
  matrix products  23.8 us (12%)
  starting transfers between devices  10.7 us (6%)
  other arithmetic  10.4 us (5%)
  waiting for transfers between devices  2.44 us (1%)
  between operations  2.11 us (1%)
    unnamed x1, blocking collectives  73.9 us
    all_gather x1, blocking collectives, per_device(): lax.all_gather(k_beacons, 'seq', axis=0, tiled=True)  22 us
    all_gather x1, blocking collectives, per_device(): lax.all_gather(v_beacons, 'seq', axis=0, tiled=True)  20 us
    ppermute x4, starting transfers between devices, passed_along(): lax.ppermute(value, axis, [(source, source + steps) for source in range(f...  10.7 us
    dot_general x4, matrix products, attend(): jnp.einsum('hqk,qhd->khd', weights, grads_out, preferred_element_type=jnp...  7.94 us
    reshape x4, local copies, waits for them, and re-layouts, per_device(): gv_parts.append(grad_v.reshape(grad_v.shape[0], -1))  6.55 us
    unnamed x63, local copies, waits for them, and re-layouts  6.15 us
    dot_general x4, matrix products, attend(): jnp.einsum('hqk,khd->qhd', weights, values, preferred_element_type=jnp.fl...  5.14 us
  transfers between devices with their start and end apart: 4, of which 1 were waited for; matrix products, arithmetic and copies ran while one was open for 6% of the time, Pallas kernels for 0%

commit v1 on v0

v1 whole, which is shorter than its diff:
```python
import functools
import math

import jax
import jax.numpy as jnp
from jax import lax
from jax.experimental import pallas as pl
from jax.experimental.pallas import tpu as pltpu
from jax.sharding import PartitionSpec as P

HEAD_DIM = 128
PAD = 16
MESH = pl.DeviceIdType.MESH
F32 = jnp.float32
BF16 = jnp.bfloat16


def dot(a, b, ca, cb):
    return lax.dot_general(a, b, (((ca,), (cb,)), ((), ())), preferred_element_type=F32)


def kernel(
    n, A, B, C, heads, seg, nb, win,
    q_ref, k_ref, v_ref, d_ref, qb_ref, kb_ref, vb_ref, db_ref, mask_ref, off_ref,
    o_t, o_b, gq_t, gk_t, gv_t, gq_b, gk_b, gv_b,
    G, KB, VB, TK, TV, SK, SV, RK, RV, WK, WV, QP, DP, bias,
    R, R1, S2, R2, X2, S3, R3,
    t_s, t_r, u_s, u_r, g1s, g1r, g2s, g2r, g3s, g3r, r1s, r1r, r2s, r2r, r3s, r3r,
):
    feat = heads * HEAD_DIM
    hc = heads // C
    hw = hc // 2
    w = hw * HEAD_DIM
    cw = hc * HEAD_DIM
    ratio = seg // nb
    rows = seg + PAD
    scale = 1.0 / HEAD_DIM**0.5
    me = lax.axis_index("seq")
    c0 = lax.rem(me, 2)
    b0 = lax.rem(me // 2, B)
    a0 = me // (2 * B)

    def at(a, b, c):
        return {"seq": (a * B + b) * 2 + c}

    def remote(src, dst, ss, rs, dev):
        return pltpu.make_async_remote_copy(
            src_ref=src, dst_ref=dst, send_sem=ss, recv_sem=rs, device_id=dev, device_id_type=MESH
        )

    zdev = [None] + [at(lax.rem(a0 + d, A), b0, c0) for d in range(1, A)]
    ydev = [None] + [at(a0, lax.rem(b0 + d, B), c0) for d in range(1, B)]
    cdev = at(a0, b0, 1 - c0)

    barrier = pltpu.get_barrier_semaphore()
    for dev in zdev[1:] + ydev[1:] + [cdev]:
        pl.semaphore_signal(barrier, inc=1, device_id=dev, device_id_type=MESH)

    @pl.when(me > 0)
    def _():
        pl.semaphore_signal(barrier, inc=1, device_id={"seq": me - 1}, device_id_type=MESH)

    @pl.when(me < n - 1)
    def _():
        pl.semaphore_signal(barrier, inc=1, device_id={"seq": me + 1}, device_id_type=MESH)

    for c in range(C):
        parts = []
        for half in range(2):
            cols = slice(c * cw + half * w, c * cw + (half + 1) * w)
            parts += [kb_ref[:, cols].astype(F32), vb_ref[:, cols].astype(F32)]
        G[c0, b0, a0, c] = jnp.concatenate(parts, axis=0).astype(BF16)

    pl.semaphore_wait(barrier, A + B + 1 - (me == 0).astype(jnp.int32) - (me == n - 1).astype(jnp.int32))

    for d in range(1, A):
        remote(G.at[c0, b0, a0], G.at[c0, b0, a0], g1s.at[d], g1r.at[d], zdev[d]).start()

    def tail(x, c):
        src, dst = ((k_ref, TK), (v_ref, TV))[x]
        cols = pl.ds(c * cw, cw)
        return remote(
            src.at[pl.ds(seg - win, win), cols], dst.at[:, cols], t_s.at[x, c], t_r.at[x, c], {"seq": lax.rem(me + 1, n)}
        )

    def back(x, c):
        src, dst = ((SK, RK), (SV, RV))[x]
        cols = pl.ds(c * cw, cw)
        return remote(
            src.at[:, cols], dst.at[:, cols], u_s.at[x, c], u_r.at[x, c], {"seq": lax.rem(me + n - 1, n)}
        )

    @pl.when(me < n - 1)
    def _():
        for c in range(C):
            tail(0, c).start()
            tail(1, c).start()

    @pl.when(me == 0)
    def _():
        TK[...] = jnp.zeros_like(TK)
        TV[...] = jnp.zeros_like(TV)

    @pl.when(me == n - 1)
    def _():
        RK[...] = jnp.zeros_like(RK)
        RV[...] = jnp.zeros_like(RV)

    zpad = jnp.zeros((PAD - nb, feat), F32)
    QP[...] = jnp.concatenate([qb_ref[...].astype(F32), zpad], axis=0).astype(BF16)
    DP[...] = jnp.concatenate([db_ref[...].astype(F32), zpad], axis=0).astype(BF16)

    NEG = -1e30

    def ids(width):
        return (
            lax.broadcasted_iota(jnp.int32, (rows, width), 0),
            lax.broadcasted_iota(jnp.int32, (rows, width), 1),
        )

    r, u = ids(win)
    ok = (r < seg) & (u > r) & (me >= 1)
    bias[:, :win] = jnp.where(ok, 0.0, NEG)
    r, u = ids(seg)
    limit = jnp.where(r < seg, r, -1)
    for b in range(nb):
        limit = jnp.where(r == seg + b, b * ratio + off_ref[b], limit)
    low = jnp.where(r < seg, r - win, -1)
    bias[:, win : win + seg] = jnp.where((u <= limit) & (u > low), 0.0, NEG)
    r, u = ids(n * nb)
    slot = u // nb
    half_n = n // 2
    owner = ((slot % A) * B + (slot % half_n) // A) * 2 + slot // half_n
    one = owner[:1]
    opened = jnp.zeros((1, n * nb), jnp.int32)
    for j in range(n):
        opened = jnp.where(one == j, mask_ref[0, j], opened)
    opened = jnp.where(one < me, opened, 0)
    earlier = jnp.broadcast_to(opened, (rows, n * nb)) == 1
    mine = (owner == me) & (r >= seg) & (u % nb <= r - seg)
    bias[:, win + seg :] = jnp.where((earlier | mine) & (r < seg + nb), 0.0, NEG)

    for d in range(1, A):
        remote(G.at[c0, b0, a0], G.at[c0, b0, lax.rem(a0 + A - d, A)], g1s.at[d], g1r.at[d], zdev[d]).wait_recv()
    for d in range(1, B):
        remote(G.at[c0, b0], G.at[c0, b0], g2s.at[d], g2r.at[d], ydev[d]).start()
    for d in range(1, B):
        remote(G.at[c0, b0], G.at[c0, lax.rem(b0 + B - d, B)], g2s.at[d], g2r.at[d], ydev[d]).wait_recv()
    remote(G.at[c0], G.at[c0], g3s.at[0], g3r.at[0], cdev).start()
    remote(G.at[c0], G.at[1 - c0], g3s.at[0], g3r.at[0], cdev).wait_recv()

    def assemble(m, carry):
        for c in range(C):
            for half in range(2):
                cols = slice(c * cw + half * w, c * cw + (half + 1) * w)
                got = []
                for i in range(PAD // nb):
                    s = m * (PAD // nb) + i
                    got.append(
                        G[s // half_n, (s % half_n) // A, s % A, c, half * 8 : half * 8 + 8, :].astype(F32)
                    )
                at_rows = pl.ds(pl.multiple_of(m * PAD, PAD), PAD)
                KB[at_rows, cols] = jnp.concatenate([x[:nb] for x in got], axis=0).astype(BF16)
                VB[at_rows, cols] = jnp.concatenate([x[nb:] for x in got], axis=0).astype(BF16)
        return carry

    lax.fori_loop(0, n * nb // PAD, assemble, 0)

    c_exp = scale * math.log2(math.e)

    def head(c, l):
        h = c * hc + l
        cols = pl.ds(pl.multiple_of(h * HEAD_DIM, HEAD_DIM), HEAD_DIM)
        q = jnp.concatenate([q_ref[:, cols], QP[:, cols]], axis=0)
        d = jnp.concatenate([d_ref[:, cols], DP[:, cols]], axis=0)
        kk = jnp.concatenate([TK[:, cols], k_ref[:, cols], KB[:, cols]], axis=0)
        vv = jnp.concatenate([TV[:, cols], v_ref[:, cols], VB[:, cols]], axis=0)
        s = dot(q, kk, 1, 1) + bias[...]
        gp = dot(d, vv, 1, 1)
        e = jnp.exp2((s - jnp.max(s, axis=1, keepdims=True)) * c_exp)
        p = e * (1.0 / jnp.sum(e, axis=1, keepdims=True))
        wt = p.astype(BF16)
        o = dot(wt, vv, 1, 0).astype(BF16)
        delta = jnp.sum(d.astype(F32) * o.astype(F32), axis=1, keepdims=True)
        ds = (p * (gp - delta)).astype(BF16)
        gq = (dot(ds, kk, 1, 0) * scale).astype(BF16)
        gv = dot(wt, d, 0, 0)
        gk = dot(ds, q, 0, 0) * scale
        o_t[:, cols] = o[:seg]
        o_b[:, cols] = o[seg : seg + nb]
        gq_t[:, cols] = gq[:seg]
        gq_b[:, cols] = gq[seg : seg + nb]
        mid = seg
        SK[:, cols] = gk[:win].astype(BF16)
        SV[:, cols] = gv[:win].astype(BF16)
        gk_t[: seg - win, cols] = gk[win:mid].astype(BF16)
        gv_t[: seg - win, cols] = gv[win:mid].astype(BF16)
        WK[:, cols] = gk[mid : win + seg]
        WV[:, cols] = gv[mid : win + seg]
        half = l // hw
        rcols = pl.ds(pl.multiple_of((l % hw) * HEAD_DIM, HEAD_DIM), HEAD_DIM)
        rrows = pl.ds(pl.multiple_of(half * 8, 8), 8)
        for sl in range(n):
            lo = win + seg + sl * nb
            both = jnp.concatenate([gk[lo : lo + nb], gv[lo : lo + nb]], axis=0)
            R[c, sl // half_n, (sl % half_n) // A, sl % A, rrows, rcols] = both

    def red1(c):
        return remote(R.at[c, 1 - c0], R1.at[c], r1s.at[c], r1r.at[c], cdev)

    def red2(c, d):
        return remote(S2.at[c, lax.rem(b0 + d, B)], R2.at[c, d], r2s.at[c, d], r2r.at[c, d], ydev[d])

    def red3(c, d):
        return remote(S3.at[c, lax.rem(a0 + d, A)], R3.at[c, d], r3s.at[c, d], r3r.at[c, d], zdev[d])

    def step1(c):
        red1(c).wait_recv()
        for b in range(B):
            tot = R1[c, b] + R[c, c0, b]
            R1[c, b] = tot
            S2[c, b] = tot.astype(BF16)
        for d in range(1, B):
            red2(c, d).start()

    def step2(c):
        tot = R1[c, b0]
        for d in range(1, B):
            red2(c, d).wait_recv()
            tot = tot + R2[c, d].astype(F32)
        X2[c] = tot
        S3[c] = tot.astype(BF16)
        for d in range(1, A):
            red3(c, d).start()

    def step3(c):
        tot = X2[c, a0]
        for d in range(1, A):
            red3(c, d).wait_recv()
            tot = tot + R3[c, d].astype(F32)
        for half in range(2):
            cols = slice(c * cw + half * w, c * cw + (half + 1) * w)
            gk_b[:, cols] = tot[half * 8 : half * 8 + nb].astype(BF16)
            gv_b[:, cols] = tot[half * 8 + nb : half * 8 + 8].astype(BF16)

    for c in range(C):

        @pl.when(me > 0)
        def _():
            tail(0, c).wait_recv()
            tail(1, c).wait_recv()

        def one_head(l, carry):
            head(c, l)
            return carry

        lax.fori_loop(0, hc, one_head, 0, unroll=UNROLL)

        red1(c).start()

        @pl.when(me > 0)
        def _():
            back(0, c).start()
            back(1, c).start()

        if c >= 1:
            step1(c - 1)
        if c >= 2:
            step2(c - 2)

    step1(C - 1)
    if C >= 2:
        step2(C - 2)
    step2(C - 1)

    for c in range(C):

        @pl.when(me < n - 1)
        def _():
            back(0, c).wait_recv()
            back(1, c).wait_recv()

        cols = slice(c * cw, (c + 1) * cw)
        gk_t[seg - win :, cols] = (WK[:, cols] + RK[:, cols].astype(F32)).astype(BF16)
        gv_t[seg - win :, cols] = (WV[:, cols] + RV[:, cols].astype(F32)).astype(BF16)

    for c in range(C):
        step3(c)

    for d in range(1, A):
        remote(G.at[c0, b0, a0], G.at[c0, b0, a0], g1s.at[d], g1r.at[d], zdev[d]).wait_send()
    for d in range(1, B):
        remote(G.at[c0, b0], G.at[c0, b0], g2s.at[d], g2r.at[d], ydev[d]).wait_send()
    remote(G.at[c0], G.at[c0], g3s.at[0], g3r.at[0], cdev).wait_send()
    for c in range(C):
        red1(c).wait_send()
        for d in range(1, B):
            red2(c, d).wait_send()
        for d in range(1, A):
            red3(c, d).wait_send()

        @pl.when(me < n - 1)
        def _():
            tail(0, c).wait_send()
            tail(1, c).wait_send()

        @pl.when(me > 0)
        def _():
            back(0, c).wait_send()
            back(1, c).wait_send()


UNROLL = 2


def per_device(n, q, k, v, dout, qb, kb, vb, db, mask, off):
    seg, feat = q.shape
    nb = qb.shape[0]
    win = seg // 2
    heads = feat // HEAD_DIM
    chips = n // 2
    B = 2 ** (int(math.log2(chips)) // 2)
    A = chips // B
    C = 4
    w = heads // C // 2 * HEAD_DIM
    keys = win + seg + n * nb
    vm = pltpu.VMEM
    dma = pltpu.SemaphoreType.DMA
    scratch = [
        vm((2, B, A, C, 16, w), BF16),
        vm((n * nb, feat), BF16),
        vm((n * nb, feat), BF16),
    ]
    scratch += [vm((win, feat), BF16)] * 6
    scratch += [vm((seg - win, feat), F32)] * 2
    scratch += [vm((PAD, feat), BF16)] * 2
    scratch += [vm((seg + PAD, keys), F32)]
    scratch += [
        vm((C, 2, B, A, 16, w), F32),
        vm((C, B, A, 16, w), F32),
        vm((C, B, A, 16, w), BF16),
        vm((C, B, A, 16, w), BF16),
        vm((C, A, 16, w), F32),
        vm((C, A, 16, w), BF16),
        vm((C, A, 16, w), BF16),
    ]
    scratch += [dma((2, C))] * 4 + [dma((A,))] * 2 + [dma((B,))] * 2 + [dma((1,))] * 2
    scratch += [dma((C,))] * 2 + [dma((C, B))] * 2 + [dma((C, A))] * 2
    big = jax.ShapeDtypeStruct((seg, feat), BF16)
    small = jax.ShapeDtypeStruct((nb, feat), BF16)
    vspec = pl.BlockSpec(memory_space=pltpu.VMEM)
    sspec = pl.BlockSpec(memory_space=pltpu.SMEM)
    macs = (seg + PAD) * keys * feat * 5
    return pl.pallas_call(
        functools.partial(kernel, n, A, B, C, heads, seg, nb, win),
        out_shape=(big, small, big, big, big, small, small, small),
        in_specs=[vspec] * 8 + [sspec] * 2,
        out_specs=(vspec,) * 8,
        scratch_shapes=scratch,
        cost_estimate=pl.CostEstimate(
            flops=2 * macs, bytes_accessed=8 * seg * feat * 2, transcendentals=(seg + PAD) * keys * heads
        ),
        compiler_params=pltpu.CompilerParams(
            collective_id=0, has_side_effects=True, vmem_limit_bytes=56 * 1024 * 1024
        ),
    )(q, k, v, dout, qb, kb, vb, db, mask, off)


def solution(mesh):
    rows = P(("groups", "seq"), None)
    return jax.shard_map(
        functools.partial(per_device, mesh.shape["seq"]),
        mesh=mesh,
        in_specs=(rows,) * 9 + (P(("groups", "seq")),),
        out_specs=(rows,) * 8,
        check_vma=False,
    )
```

time: 193 us -> 51.3 us (0.27)
  blocking collectives: 116 us -> 0 us
  Pallas kernels: 0 us -> 42.4 us
  matrix products: 23.8 us -> 0 us
  local copies, waits for them, and re-layouts: 26.5 us -> 7.86 us
  starting transfers between devices: 10.7 us -> 0 us
  other arithmetic: 10.4 us -> 0 us
  waiting for transfers between devices: 2.44 us -> 0 us
    unnamed x1 -> x0, blocking collectives: 73.9 us -> none
    pallas_call x0 -> x1, Pallas kernels: none -> 42.4 us  [per_device(): pl.pallas_call(functools.partial(kernel, n, A, B, C, heads, seg, nb, win)...]
    all_gather x2 -> x0, blocking collectives: 42.1 us -> none  [the longest x1 22 us: per_device(): lax.all_gather(k_beacons, 'seq', axis=0, tiled=True)]
    dot_general x20 -> x0, matrix products: 19.4 us -> none  [the longest x4 7.94 us: attend(): jnp.einsum('hqk,qhd->khd', weights, grads_out, preferred_element_type=jnp...]
    ppermute x4 -> x0, starting transfers between devices: 10.7 us -> none  [passed_along(): lax.ppermute(value, axis, [(source, source + steps) for source in range(f...]
    reshape x17 -> x0, local copies, waits for them, and re-layouts: 9.55 us -> none  [the longest x4 6.55 us: per_device(): gv_parts.append(grad_v.reshape(grad_v.shape[0], -1))]
    slice x12 -> x0, local copies, waits for them, and re-layouts: 8.95 us -> none  [the longest x4 2.25 us: heads_view(): matrix[:, col_lo:col_lo + block_heads * HEAD_DIM]]
    concatenate x6 -> x0, other arithmetic: 6.48 us -> none  [the longest x1 1.64 us: per_device(): key_rows = jnp.concatenate([tail_k, k_tokens, every_bk], axis=0)]
  transfers between devices with their start and end apart: 4 -> 0, of which waited for: 1 -> 0; matrix products, arithmetic and copies ran while one was open for 6% -> 0% of each run, Pallas kernels for 0% -> 0%
where the time goes in v1:
time: 51.3 us; the launch traced here: 50.9 us
  Pallas kernels  42.4 us (83%)
  local copies, waits for them, and re-layouts  7.86 us (15%)
  between operations  0.67 us (1%)
    pallas_call x1, Pallas kernels, per_device(): pl.pallas_call(functools.partial(kernel, n, A, B, C, heads, seg, nb, win)...  42.4 us
    unnamed x22, local copies, waits for them, and re-layouts  7.86 us

profile of v1, /device:TPU:0, one launch (start us, length us, event | category | flops | bytes accessed | tf_op | source)
XLA Modules:
  0.0 50.9 jit_solution(2463490712498914495)
XLA Ops:
  0.6 42.4 %shard_map.161 = (bf16[128,2048]{1,0:T(8,128)(2,1)}, bf16[4,2048]{1,0:T(4,128)(2,1)}, bf16[128,2048]{1,0:T(8,128)(2,1)}, bf16[128,2048]{1,0:T(8,128)(2,1)}, bf16...) custom-call(bf16[128,2048]{1,0:T(8,128)(2,1)} %q_ref.1, ...), custom_call_target="tpu_custom_call" | custom-call | flops 754974720 | bytes 4194304 | tf_op jit(solution)/shard_map/pallas_call | solution.py:354
  43.0 0.0 copy-start.6
  43.0 0.0 copy-start.2
  43.0 1.9 %copy.26 = bf16[128,2048]{1,0:T(8,128)(2,1)} copy(bf16[128,2048]{1,0:T(8,128)(2,1)} %get-tuple-element.16) | data formatting | bytes 1048576
  45.0 0.0 copy-done.6
  45.0 0.6 %copy.27 = bf16[4,2048]{1,0:T(4,128)(2,1)} copy(bf16[4,2048]{1,0:T(4,128)(2,1)S(1)} %copy-done.6) | data formatting | bytes 32768
  45.6 0.0 copy-done.2
  45.6 0.0 copy-start.1
  45.6 0.8 %copy.28 = bf16[128,2048]{1,0:T(8,128)(2,1)} copy(bf16[128,2048]{1,0:T(8,128)(2,1)S(1)} %copy-done.2) | data formatting | bytes 1048576
  46.4 0.4 copy-done.1
  46.8 0.0 copy-start
  46.8 0.8 %copy.29 = bf16[128,2048]{1,0:T(8,128)(2,1)} copy(bf16[128,2048]{1,0:T(8,128)(2,1)S(1)} %copy-done.1) | data formatting | bytes 1048576
  47.6 0.4 copy-done
  48.0 0.0 copy-start.5
  48.0 0.8 %copy.30 = bf16[128,2048]{1,0:T(8,128)(2,1)} copy(bf16[128,2048]{1,0:T(8,128)(2,1)S(1)} %copy-done) | data formatting | bytes 1048576
  48.8 0.0 copy-done.5
  48.8 0.0 copy-start.4
  48.8 0.6 %copy.31 = bf16[4,2048]{1,0:T(4,128)(2,1)} copy(bf16[4,2048]{1,0:T(4,128)(2,1)S(1)} %copy-done.5) | data formatting | bytes 32768
  49.4 0.1 copy-done.4
  49.6 0.0 copy-start.3
  49.6 0.6 %copy.32 = bf16[4,2048]{1,0:T(4,128)(2,1)} copy(bf16[4,2048]{1,0:T(4,128)(2,1)S(1)} %copy-done.4) | data formatting | bytes 32768
  50.2 0.1 copy-done.3
  50.3 0.6 %copy.33 = bf16[4,2048]{1,0:T(4,128)(2,1)} copy(bf16[4,2048]{1,0:T(4,128)(2,1)S(1)} %copy-done.3) | data formatting | bytes 32768
Async XLA Ops:
  43.0 2.0 %copy-start.6 = (bf16[4,2048]{1,0:T(4,128)(2,1)S(1)}, bf16[4,2048]{1,0:T(4,128)(2,1)}, u32[]{:S(2)}) copy-start(bf16[4,2048]{1,0:T(4,128)(2,1)} %get-tuple-element.17) | copy-start | bytes 49156
  43.0 2.6 %copy-start.2 = (bf16[128,2048]{1,0:T(8,128)(2,1)S(1)}, bf16[128,2048]{1,0:T(8,128)(2,1)}, u32[]{:S(2)}) copy-start(bf16[128,2048]{1,0:T(8,128)(2,1)} %get-tuple-element.18) | copy-start | bytes 1572868
  45.6 1.2 %copy-start.1 = (bf16[128,2048]{1,0:T(8,128)(2,1)S(1)}, bf16[128,2048]{1,0:T(8,128)(2,1)}, u32[]{:S(2)}) copy-start(bf16[128,2048]{1,0:T(8,128)(2,1)} %get-tuple-element.19) | copy-start | bytes 1572868
  46.8 1.2 %copy-start = (bf16[128,2048]{1,0:T(8,128)(2,1)S(1)}, bf16[128,2048]{1,0:T(8,128)(2,1)}, u32[]{:S(2)}) copy-start(bf16[128,2048]{1,0:T(8,128)(2,1)} %get-tuple-element.20) | copy-start | bytes 1572868
  48.0 0.8 %copy-start.5 = (bf16[4,2048]{1,0:T(4,128)(2,1)S(1)}, bf16[4,2048]{1,0:T(4,128)(2,1)}, u32[]{:S(2)}) copy-start(bf16[4,2048]{1,0:T(4,128)(2,1)} %get-tuple-element.21) | copy-start | bytes 49156
  48.8 0.7 %copy-start.4 = (bf16[4,2048]{1,0:T(4,128)(2,1)S(1)}, bf16[4,2048]{1,0:T(4,128)(2,1)}, u32[]{:S(2)}) copy-start(bf16[4,2048]{1,0:T(4,128)(2,1)} %get-tuple-element.22) | copy-start | bytes 49156
  49.6 0.7 %copy-start.3 = (bf16[4,2048]{1,0:T(4,128)(2,1)S(1)}, bf16[4,2048]{1,0:T(4,128)(2,1)}, u32[]{:S(2)}) copy-start(bf16[4,2048]{1,0:T(4,128)(2,1)} %get-tuple-element.23) | copy-start | bytes 49156

commit v2 on v1

--- a/solution.py
+++ b/solution.py
@@ -33,6 +33,7 @@
     w = hw * HEAD_DIM
     cw = hc * HEAD_DIM
     ratio = seg // nb
+    cg = C // GC
     rows = seg + PAD
     scale = 1.0 / HEAD_DIM**0.5
     me = lax.axis_index("seq")
@@ -69,12 +70,26 @@
         for half in range(2):
             cols = slice(c * cw + half * w, c * cw + (half + 1) * w)
             parts += [kb_ref[:, cols].astype(F32), vb_ref[:, cols].astype(F32)]
-        G[c0, b0, a0, c] = jnp.concatenate(parts, axis=0).astype(BF16)
+        G[c // cg, c0, b0, a0, c % cg] = jnp.concatenate(parts, axis=0).astype(BF16)
 
     pl.semaphore_wait(barrier, A + B + 1 - (me == 0).astype(jnp.int32) - (me == n - 1).astype(jnp.int32))
 
-    for d in range(1, A):
-        remote(G.at[c0, b0, a0], G.at[c0, b0, a0], g1s.at[d], g1r.at[d], zdev[d]).start()
+    def hop1(g, d, src=0):
+        return remote(
+            G.at[g, c0, b0, a0], G.at[g, c0, b0, lax.rem(a0 + A - src, A)], g1s.at[g, d], g1r.at[g, d], zdev[d]
+        )
+
+    def hop2(g, d, src=0):
+        return remote(
+            G.at[g, c0, b0], G.at[g, c0, lax.rem(b0 + B - src, B)], g2s.at[g, d], g2r.at[g, d], ydev[d]
+        )
+
+    def hop3(g, src=0):
+        return remote(G.at[g, c0], G.at[g, lax.rem(c0 + src, 2)], g3s.at[g], g3r.at[g], cdev)
+
+    for g in range(GC):
+        for d in range(1, A):
+            hop1(g, d).start()
 
     def tail(x, c):
         src, dst = ((k_ref, TK), (v_ref, TV))[x]
@@ -90,11 +105,13 @@
             src.at[:, cols], dst.at[:, cols], u_s.at[x, c], u_r.at[x, c], {"seq": lax.rem(me + n - 1, n)}
         )
 
-    @pl.when(me < n - 1)
-    def _():
-        for c in range(C):
+    def tail_start(c):
+        @pl.when(me < n - 1)
+        def _():
             tail(0, c).start()
             tail(1, c).start()
+
+    tail_start(0)
 
     @pl.when(me == 0)
     def _():
@@ -140,31 +157,37 @@
     mine = (owner == me) & (r >= seg) & (u % nb <= r - seg)
     bias[:, win + seg :] = jnp.where((earlier | mine) & (r < seg + nb), 0.0, NEG)
 
-    for d in range(1, A):
-        remote(G.at[c0, b0, a0], G.at[c0, b0, lax.rem(a0 + A - d, A)], g1s.at[d], g1r.at[d], zdev[d]).wait_recv()
-    for d in range(1, B):
-        remote(G.at[c0, b0], G.at[c0, b0], g2s.at[d], g2r.at[d], ydev[d]).start()
-    for d in range(1, B):
-        remote(G.at[c0, b0], G.at[c0, lax.rem(b0 + B - d, B)], g2s.at[d], g2r.at[d], ydev[d]).wait_recv()
-    remote(G.at[c0], G.at[c0], g3s.at[0], g3r.at[0], cdev).start()
-    remote(G.at[c0], G.at[1 - c0], g3s.at[0], g3r.at[0], cdev).wait_recv()
-
-    def assemble(m, carry):
-        for c in range(C):
+    for g in range(GC):
+        for d in range(1, A):
+            hop1(g, d, d).wait_recv()
+        for d in range(1, B):
+            hop2(g, d).start()
+    for c in range(1, cg):
+        tail_start(c)
+
+    def assemble(g, m, carry):
+        for c in range(g * cg, (g + 1) * cg):
             for half in range(2):
                 cols = slice(c * cw + half * w, c * cw + (half + 1) * w)
                 got = []
                 for i in range(PAD // nb):
                     s = m * (PAD // nb) + i
                     got.append(
-                        G[s // half_n, (s % half_n) // A, s % A, c, half * 8 : half * 8 + 8, :].astype(F32)
+                        G[g, s // half_n, (s % half_n) // A, s % A, c % cg, half * 8 : half * 8 + 8, :].astype(F32)
                     )
                 at_rows = pl.ds(pl.multiple_of(m * PAD, PAD), PAD)
                 KB[at_rows, cols] = jnp.concatenate([x[:nb] for x in got], axis=0).astype(BF16)
                 VB[at_rows, cols] = jnp.concatenate([x[nb:] for x in got], axis=0).astype(BF16)
         return carry
 
-    lax.fori_loop(0, n * nb // PAD, assemble, 0)
+    def pass_on(g):
+        for d in range(1, B):
+            hop2(g, d, d).wait_recv()
+        hop3(g).start()
+
+    def arrived(g):
+        hop3(g, 1).wait_recv()
+        lax.fori_loop(0, n * nb // PAD, functools.partial(assemble, g), 0)
 
     c_exp = scale * math.log2(math.e)
 
@@ -243,7 +266,12 @@
             gk_b[:, cols] = tot[half * 8 : half * 8 + nb].astype(BF16)
             gv_b[:, cols] = tot[half * 8 + nb : half * 8 + 8].astype(BF16)
 
+    pass_on(0)
+    for c in range(cg, C):
+        tail_start(c)
     for c in range(C):
+        if c % cg == 0:
+            arrived(c // cg)
 
         @pl.when(me > 0)
         def _():
@@ -263,6 +291,8 @@
             back(0, c).start()
             back(1, c).start()
 
+        if c % cg == 0 and c // cg + 1 < GC:
+            pass_on(c // cg + 1)
         if c >= 1:
             step1(c - 1)
         if c >= 2:
@@ -287,11 +317,12 @@
     for c in range(C):
         step3(c)
 
-    for d in range(1, A):
-        remote(G.at[c0, b0, a0], G.at[c0, b0, a0], g1s.at[d], g1r.at[d], zdev[d]).wait_send()
-    for d in range(1, B):
-        remote(G.at[c0, b0], G.at[c0, b0], g2s.at[d], g2r.at[d], ydev[d]).wait_send()
-    remote(G.at[c0], G.at[c0], g3s.at[0], g3r.at[0], cdev).wait_send()
+    for g in range(GC):
+        for d in range(1, A):
+            hop1(g, d).wait_send()
+        for d in range(1, B):
+            hop2(g, d).wait_send()
+        hop3(g).wait_send()
     for c in range(C):
         red1(c).wait_send()
         for d in range(1, B):
@@ -310,7 +341,21 @@
             back(1, c).wait_send()
 
 
-UNROLL = 2
+def hand_over(*refs):
+    src, dst, held, ins, outs = refs[:8], refs[8:16], refs[16:24], refs[24], refs[25]
+    first = [pltpu.make_async_copy(src[i], held[i], ins.at[i]) for i in range(8)]
+    second = [pltpu.make_async_copy(held[i], dst[i], outs.at[i]) for i in range(8)]
+    for copy in first:
+        copy.start()
+    for i in range(8):
+        first[i].wait()
+        second[i].start()
+    for copy in second:
+        copy.wait()
+
+
+UNROLL = 4
+GC = 2
 
 
 def per_device(n, q, k, v, dout, qb, kb, vb, db, mask, off):
@@ -327,7 +372,7 @@
     vm = pltpu.VMEM
     dma = pltpu.SemaphoreType.DMA
     scratch = [
-        vm((2, B, A, C, 16, w), BF16),
+        vm((GC, 2, B, A, C // GC, 16, w), BF16),
         vm((n * nb, feat), BF16),
         vm((n * nb, feat), BF16),
     ]
@@ -344,14 +389,14 @@
         vm((C, A, 16, w), BF16),
         vm((C, A, 16, w), BF16),
     ]
-    scratch += [dma((2, C))] * 4 + [dma((A,))] * 2 + [dma((B,))] * 2 + [dma((1,))] * 2
+    scratch += [dma((2, C))] * 4 + [dma((GC, A))] * 2 + [dma((GC, B))] * 2 + [dma((GC,))] * 2
     scratch += [dma((C,))] * 2 + [dma((C, B))] * 2 + [dma((C, A))] * 2
     big = jax.ShapeDtypeStruct((seg, feat), BF16)
     small = jax.ShapeDtypeStruct((nb, feat), BF16)
     vspec = pl.BlockSpec(memory_space=pltpu.VMEM)
     sspec = pl.BlockSpec(memory_space=pltpu.SMEM)
     macs = (seg + PAD) * keys * feat * 5
-    return pl.pallas_call(
+    parts = pl.pallas_call(
         functools.partial(kernel, n, A, B, C, heads, seg, nb, win),
         out_shape=(big, small, big, big, big, small, small, small),
         in_specs=[vspec] * 8 + [sspec] * 2,
@@ -364,6 +409,16 @@
             collective_id=0, has_side_effects=True, vmem_limit_bytes=56 * 1024 * 1024
         ),
     )(q, k, v, dout, qb, kb, vb, db, mask, off)
+    aspec = pl.BlockSpec(memory_space=pl.ANY)
+    return pl.pallas_call(
+        hand_over,
+        out_shape=(big, small, big, big, big, small, small, small),
+        in_specs=[aspec] * 8,
+        out_specs=(aspec,) * 8,
+        scratch_shapes=[vm(x.shape, BF16) for x in (big, small, big, big, big, small, small, small)]
+        + [dma((8,))] * 2,
+        cost_estimate=pl.CostEstimate(flops=0, bytes_accessed=16 * seg * feat, transcendentals=0),
+    )(*parts)
 
 
 def solution(mesh):

time: 51.3 us -> 43.6 us (0.85)
  local copies, waits for them, and re-layouts: 7.86 us -> 0 us
    unnamed x22 -> x0, local copies, waits for them, and re-layouts: 7.86 us -> none
    pallas_call x0 -> x1, Pallas kernels: none -> 2.51 us  [per_device(): pl.pallas_call(hand_over, out_shape=(big, small, big, big, big, small, sm...]
    pallas_call x1, Pallas kernels: 42.4 us -> 40.3 us  [per_device(): pl.pallas_call(functools.partial(kernel, n, A, B, C, heads, seg, nb, win)...]
where the time goes in v2:
time: 43.6 us; the launch traced here: 43.4 us
  Pallas kernels  42.8 us (98%)
  between operations  0.64 us (1%)
    pallas_call x1, Pallas kernels, per_device(): pl.pallas_call(functools.partial(kernel, n, A, B, C, heads, seg, nb, win)...  40.3 us
    pallas_call x1, Pallas kernels, per_device(): pl.pallas_call(hand_over, out_shape=(big, small, big, big, big, small, sm...  2.51 us

profile of v2, /device:TPU:0, one launch (start us, length us, event | category | flops | bytes accessed | tf_op | source)
XLA Modules:
  0.0 43.4 jit_solution(8238808226854161589)
XLA Ops:
  0.6 40.3 %shard_map.161 = (bf16[128,2048]{1,0:T(8,128)(2,1)}, bf16[4,2048]{1,0:T(4,128)(2,1)}, bf16[128,2048]{1,0:T(8,128)(2,1)}, bf16[128,2048]{1,0:T(8,128)(2,1)}, bf16...) custom-call(bf16[128,2048]{1,0:T(8,128)(2,1)} %q_ref.1, ...), custom_call_target="tpu_custom_call" | custom-call | flops 754974720 | bytes 4194304 | tf_op jit(solution)/shard_map/pallas_call | solution.py:399
  40.9 2.5 %shard_map.162 = (bf16[128,2048]{1,0:T(8,128)(2,1)}, bf16[4,2048]{1,0:T(4,128)(2,1)}, bf16[128,2048]{1,0:T(8,128)(2,1)}, bf16[128,2048]{1,0:T(8,128)(2,1)}, bf16...) custom-call(bf16[128,2048]{1,0:T(8,128)(2,1)} %get-tuple-element.16.refs_0_,, ...), custom_call_target="tpu_custom_call" | custom-call | bytes 4194304 | tf_op jit(solution)/shard_map/pallas_call | solution.py:413

commit v3 on v2

--- a/solution.py
+++ b/solution.py
@@ -20,12 +20,12 @@
 
 
 def kernel(
-    n, A, B, C, heads, seg, nb, win,
+    n, C, heads, seg, nb, win,
     q_ref, k_ref, v_ref, d_ref, qb_ref, kb_ref, vb_ref, db_ref, mask_ref, off_ref,
     o_t, o_b, gq_t, gk_t, gv_t, gq_b, gk_b, gv_b,
     G, KB, VB, TK, TV, SK, SV, RK, RV, WK, WV, QP, DP, bias,
-    R, R1, S2, R2, X2, S3, R3,
-    t_s, t_r, u_s, u_r, g1s, g1r, g2s, g2r, g3s, g3r, r1s, r1r, r2s, r2r, r3s, r3r,
+    R, R1, S2, R2,
+    t_s, t_r, u_s, u_r, g1s, g1r, g2s, g2r, r1s, r1r, r2s, r2r,
 ):
     feat = heads * HEAD_DIM
     hc = heads // C
@@ -38,23 +38,20 @@
     scale = 1.0 / HEAD_DIM**0.5
     me = lax.axis_index("seq")
     c0 = lax.rem(me, 2)
-    b0 = lax.rem(me // 2, B)
-    a0 = me // (2 * B)
-
-    def at(a, b, c):
-        return {"seq": (a * B + b) * 2 + c}
+    chips = n // 2
+    p0 = me // 2
+    cdev = {"seq": p0 * 2 + 1 - c0}
+
+    def chip(d):
+        return {"seq": lax.rem(p0 + d + chips, chips) * 2 + c0}
 
     def remote(src, dst, ss, rs, dev):
         return pltpu.make_async_remote_copy(
             src_ref=src, dst_ref=dst, send_sem=ss, recv_sem=rs, device_id=dev, device_id_type=MESH
         )
 
-    zdev = [None] + [at(lax.rem(a0 + d, A), b0, c0) for d in range(1, A)]
-    ydev = [None] + [at(a0, lax.rem(b0 + d, B), c0) for d in range(1, B)]
-    cdev = at(a0, b0, 1 - c0)
-
     barrier = pltpu.get_barrier_semaphore()
-    for dev in zdev[1:] + ydev[1:] + [cdev]:
+    for dev in [chip(d) for d in range(1, chips)] + [cdev]:
         pl.semaphore_signal(barrier, inc=1, device_id=dev, device_id_type=MESH)
 
     @pl.when(me > 0)
@@ -70,26 +67,28 @@
         for half in range(2):
             cols = slice(c * cw + half * w, c * cw + (half + 1) * w)
             parts += [kb_ref[:, cols].astype(F32), vb_ref[:, cols].astype(F32)]
-        G[c // cg, c0, b0, a0, c % cg] = jnp.concatenate(parts, axis=0).astype(BF16)
-
-    pl.semaphore_wait(barrier, A + B + 1 - (me == 0).astype(jnp.int32) - (me == n - 1).astype(jnp.int32))
-
-    def hop1(g, d, src=0):
-        return remote(
-            G.at[g, c0, b0, a0], G.at[g, c0, b0, lax.rem(a0 + A - src, A)], g1s.at[g, d], g1r.at[g, d], zdev[d]
-        )
-
-    def hop2(g, d, src=0):
-        return remote(
-            G.at[g, c0, b0], G.at[g, c0, lax.rem(b0 + B - src, B)], g2s.at[g, d], g2r.at[g, d], ydev[d]
-        )
-
-    def hop3(g, src=0):
-        return remote(G.at[g, c0], G.at[g, lax.rem(c0 + src, 2)], g3s.at[g], g3r.at[g], cdev)
-
-    for g in range(GC):
-        for d in range(1, A):
-            hop1(g, d).start()
+        G[c // cg, c0, p0, c % cg] = jnp.concatenate(parts, axis=0).astype(BF16)
+
+    pl.semaphore_wait(barrier, chips + 2 - (me == 0).astype(jnp.int32) - (me == n - 1).astype(jnp.int32))
+
+    def up(g, d):
+        return remote(G.at[g, c0, p0], G.at[g, c0, p0], g1s.at[g, d], g1r.at[g, d], chip(d))
+
+    def up_here(g, d):
+        slot = G.at[g, c0, lax.rem(p0 - d + chips, chips)]
+        return remote(slot, slot, g1s.at[g, d], g1r.at[g, d], chip(d))
+
+    def across(g, src=0):
+        return remote(G.at[g, c0], G.at[g, lax.rem(c0 + src, 2)], g2s.at[g], g2r.at[g], cdev)
+
+    def up_start(g):
+        for d in range(1, chips):
+
+            @pl.when(p0 + d < chips)
+            def _():
+                up(g, d).start()
+
+    up_start(0)
 
     def tail(x, c):
         src, dst = ((k_ref, TK), (v_ref, TV))[x]
@@ -112,6 +111,20 @@
             tail(1, c).start()
 
     tail_start(0)
+    for g in range(1, GC):
+        up_start(g)
+
+    for d in range(1, chips):
+
+        @pl.when(p0 < d)
+        def _():
+            for g in range(GC):
+                G[g, c0, p0 - d + chips] = jnp.zeros_like(G[g, c0, 0])
+
+        @pl.when(p0 + d >= chips)
+        def _():
+            for c in range(C):
+                R2[c, d] = jnp.zeros_like(R2[c, d])
 
     @pl.when(me == 0)
     def _():
@@ -146,8 +159,7 @@
     bias[:, win : win + seg] = jnp.where((u <= limit) & (u > low), 0.0, NEG)
     r, u = ids(n * nb)
     slot = u // nb
-    half_n = n // 2
-    owner = ((slot % A) * B + (slot % half_n) // A) * 2 + slot // half_n
+    owner = (slot % chips) * 2 + slot // chips
     one = owner[:1]
     opened = jnp.zeros((1, n * nb), jnp.int32)
     for j in range(n):
@@ -157,14 +169,6 @@
     mine = (owner == me) & (r >= seg) & (u % nb <= r - seg)
     bias[:, win + seg :] = jnp.where((earlier | mine) & (r < seg + nb), 0.0, NEG)
 
-    for g in range(GC):
-        for d in range(1, A):
-            hop1(g, d, d).wait_recv()
-        for d in range(1, B):
-            hop2(g, d).start()
-    for c in range(1, cg):
-        tail_start(c)
-
     def assemble(g, m, carry):
         for c in range(g * cg, (g + 1) * cg):
             for half in range(2):
@@ -173,7 +177,7 @@
                 for i in range(PAD // nb):
                     s = m * (PAD // nb) + i
                     got.append(
-                        G[g, s // half_n, (s % half_n) // A, s % A, c % cg, half * 8 : half * 8 + 8, :].astype(F32)
+                        G[g, s // chips, s % chips, c % cg, half * 8 : half * 8 + 8, :].astype(F32)
                     )
                 at_rows = pl.ds(pl.multiple_of(m * PAD, PAD), PAD)
                 KB[at_rows, cols] = jnp.concatenate([x[:nb] for x in got], axis=0).astype(BF16)
@@ -181,12 +185,16 @@
         return carry
 
     def pass_on(g):
-        for d in range(1, B):
-            hop2(g, d, d).wait_recv()
-        hop3(g).start()
+        for d in range(1, chips):
+
+            @pl.when(p0 >= d)
+            def _():
+                up_here(g, d).wait_recv()
+
+        across(g).start()
 
     def arrived(g):
-        hop3(g, 1).wait_recv()
+        across(g, 1).wait_recv()
         lax.fori_loop(0, n * nb // PAD, functools.partial(assemble, g), 0)
 
     c_exp = scale * math.log2(math.e)
@@ -226,48 +234,44 @@
         for sl in range(n):
             lo = win + seg + sl * nb
             both = jnp.concatenate([gk[lo : lo + nb], gv[lo : lo + nb]], axis=0)
-            R[c, sl // half_n, (sl % half_n) // A, sl % A, rrows, rcols] = both
+            R[c, sl // chips, sl % chips, rrows, rcols] = both
 
     def red1(c):
         return remote(R.at[c, 1 - c0], R1.at[c], r1s.at[c], r1r.at[c], cdev)
 
-    def red2(c, d):
-        return remote(S2.at[c, lax.rem(b0 + d, B)], R2.at[c, d], r2s.at[c, d], r2r.at[c, d], ydev[d])
-
-    def red3(c, d):
-        return remote(S3.at[c, lax.rem(a0 + d, A)], R3.at[c, d], r3s.at[c, d], r3r.at[c, d], zdev[d])
+    def down(c, d):
+        return remote(
+            S2.at[c, lax.rem(p0 - d + chips, chips)], R2.at[c, d], r2s.at[c, d], r2r.at[c, d], chip(-d)
+        )
 
     def step1(c):
         red1(c).wait_recv()
-        for b in range(B):
-            tot = R1[c, b] + R[c, c0, b]
-            R1[c, b] = tot
-            S2[c, b] = tot.astype(BF16)
-        for d in range(1, B):
-            red2(c, d).start()
+        tot = R1[c] + R[c, c0]
+        R1[c] = tot
+        S2[c] = tot.astype(BF16)
+        for d in range(1, chips):
+
+            @pl.when(p0 >= d)
+            def _():
+                down(c, d).start()
 
     def step2(c):
-        tot = R1[c, b0]
-        for d in range(1, B):
-            red2(c, d).wait_recv()
+        for d in range(1, chips):
+
+            @pl.when(p0 + d < chips)
+            def _():
+                down(c, d).wait_recv()
+
+        tot = R1[c, p0]
+        for d in range(1, chips):
             tot = tot + R2[c, d].astype(F32)
-        X2[c] = tot
-        S3[c] = tot.astype(BF16)
-        for d in range(1, A):
-            red3(c, d).start()
-
-    def step3(c):
-        tot = X2[c, a0]
-        for d in range(1, A):
-            red3(c, d).wait_recv()
-            tot = tot + R3[c, d].astype(F32)
         for half in range(2):
             cols = slice(c * cw + half * w, c * cw + (half + 1) * w)
             gk_b[:, cols] = tot[half * 8 : half * 8 + nb].astype(BF16)
             gv_b[:, cols] = tot[half * 8 + nb : half * 8 + 8].astype(BF16)
 
     pass_on(0)
-    for c in range(cg, C):
+    for c in range(1, C):
         tail_start(c)
     for c in range(C):
         if c % cg == 0:
@@ -295,13 +299,8 @@
             pass_on(c // cg + 1)
         if c >= 1:
             step1(c - 1)
-        if c >= 2:
-            step2(c - 2)
 
     step1(C - 1)
-    if C >= 2:
-        step2(C - 2)
-    step2(C - 1)
 
     for c in range(C):
 
@@ -315,20 +314,23 @@
         gv_t[seg - win :, cols] = (WV[:, cols] + RV[:, cols].astype(F32)).astype(BF16)
 
     for c in range(C):
-        step3(c)
+        step2(c)
 
     for g in range(GC):
-        for d in range(1, A):
-            hop1(g, d).wait_send()
-        for d in range(1, B):
-            hop2(g, d).wait_send()
-        hop3(g).wait_send()
+        for d in range(1, chips):
+
+            @pl.when(p0 + d < chips)
+            def _():
+                up(g, d).wait_send()
+
+        across(g).wait_send()
     for c in range(C):
         red1(c).wait_send()
-        for d in range(1, B):
-            red2(c, d).wait_send()
-        for d in range(1, A):
-            red3(c, d).wait_send()
+        for d in range(1, chips):
+
+            @pl.when(p0 >= d)
+            def _():
+                down(c, d).wait_send()
 
         @pl.when(me < n - 1)
         def _():
@@ -364,15 +366,13 @@
     win = seg // 2
     heads = feat // HEAD_DIM
     chips = n // 2
-    B = 2 ** (int(math.log2(chips)) // 2)
-    A = chips // B
     C = 4
     w = heads // C // 2 * HEAD_DIM
     keys = win + seg + n * nb
     vm = pltpu.VMEM
     dma = pltpu.SemaphoreType.DMA
     scratch = [
-        vm((GC, 2, B, A, C // GC, 16, w), BF16),
+        vm((GC, 2, chips, C // GC, 16, w), BF16),
         vm((n * nb, feat), BF16),
         vm((n * nb, feat), BF16),
     ]
@@ -381,23 +381,20 @@
     scratch += [vm((PAD, feat), BF16)] * 2
     scratch += [vm((seg + PAD, keys), F32)]
     scratch += [
-        vm((C, 2, B, A, 16, w), F32),
-        vm((C, B, A, 16, w), F32),
-        vm((C, B, A, 16, w), BF16),
-        vm((C, B, A, 16, w), BF16),
-        vm((C, A, 16, w), F32),
-        vm((C, A, 16, w), BF16),
-        vm((C, A, 16, w), BF16),
+        vm((C, 2, chips, 16, w), F32),
+        vm((C, chips, 16, w), F32),
+        vm((C, chips, 16, w), BF16),
+        vm((C, chips, 16, w), BF16),
     ]
-    scratch += [dma((2, C))] * 4 + [dma((GC, A))] * 2 + [dma((GC, B))] * 2 + [dma((GC,))] * 2
-    scratch += [dma((C,))] * 2 + [dma((C, B))] * 2 + [dma((C, A))] * 2
+    scratch += [dma((2, C))] * 4 + [dma((GC, chips))] * 2 + [dma((GC,))] * 2
+    scratch += [dma((C,))] * 2 + [dma((C, chips))] * 2
     big = jax.ShapeDtypeStruct((seg, feat), BF16)
     small = jax.ShapeDtypeStruct((nb, feat), BF16)
     vspec = pl.BlockSpec(memory_space=pltpu.VMEM)
     sspec = pl.BlockSpec(memory_space=pltpu.SMEM)
     macs = (seg + PAD) * keys * feat * 5
     parts = pl.pallas_call(
-        functools.partial(kernel, n, A, B, C, heads, seg, nb, win),
+        functools.partial(kernel, n, C, heads, seg, nb, win),
         out_shape=(big, small, big, big, big, small, small, small),
         in_specs=[vspec] * 8 + [sspec] * 2,
         out_specs=(vspec,) * 8,

time: 43.6 us -> 37.7 us (0.86)
  Pallas kernels: 42.8 us -> 36.9 us
    pallas_call x1, Pallas kernels: 40.3 us -> 34.4 us  [per_device(): pl.pallas_call(functools.partial(kernel, n, C, heads, seg, nb, win), out_...]
where the time goes in v3:
time: 37.7 us; the launch traced here: 37.5 us
  Pallas kernels  36.9 us (98%)
  between operations  0.64 us (2%)
    pallas_call x1, Pallas kernels, per_device(): pl.pallas_call(functools.partial(kernel, n, C, heads, seg, nb, win), out_...  34.4 us
    pallas_call x1, Pallas kernels, per_device(): pl.pallas_call(hand_over, out_shape=(big, small, big, big, big, small, sm...  2.51 us

profile of v3, /device:TPU:0, one launch (start us, length us, event | category | flops | bytes accessed | tf_op | source)
XLA Modules:
  0.0 37.5 jit_solution(12743198261706850998)
XLA Ops:
  0.6 34.4 %shard_map.161 = (bf16[128,2048]{1,0:T(8,128)(2,1)}, bf16[4,2048]{1,0:T(4,128)(2,1)}, bf16[128,2048]{1,0:T(8,128)(2,1)}, bf16[128,2048]{1,0:T(8,128)(2,1)}, bf16...) custom-call(bf16[128,2048]{1,0:T(8,128)(2,1)} %q_ref.1, ...), custom_call_target="tpu_custom_call" | custom-call | flops 754974720 | bytes 4194304 | tf_op jit(solution)/shard_map/pallas_call | solution.py:396
  35.0 2.5 %shard_map.162 = (bf16[128,2048]{1,0:T(8,128)(2,1)}, bf16[4,2048]{1,0:T(4,128)(2,1)}, bf16[128,2048]{1,0:T(8,128)(2,1)}, bf16[128,2048]{1,0:T(8,128)(2,1)}, bf16...) custom-call(bf16[128,2048]{1,0:T(8,128)(2,1)} %get-tuple-element.16.refs_0_,, ...), custom_call_target="tpu_custom_call" | custom-call | bytes 4194304 | tf_op jit(solution)/shard_map/pallas_call | solution.py:410
